TPU v7x, 256 devices: a whole 4x4x8 slice. The times are simulated.
256 devices in a mesh: tx: 8 (over z), ty: 32 (over y, x, core).
Axes of the slice: x: 4, y: 4, z: 8, core: 2. Of those that a mesh axis runs over, the one named last changes fastest.
Arguments:
- signal: bfloat16 [262144, 256], P(('tx', 'ty')), may hold values from -6 to 6
- sketch: bfloat16 [64, 16384], replicated, may hold values from -0.046875 to 0.046875
Outputs:
- basis_t: float32 [64, 262144], P(None, ('tx', 'ty'))
- projected: float32 [64, 16384], P(None, ('tx', 'ty'))
All inputs are finite; a program needn't handle non-finite values.
Results may differ from a plain program's by a relative error of at most 0.00071.
Values may be sent and summed in bfloat16 or wider, within the bound.
A program may use at most 128 MiB of HBM per device.

v0:
```python
import math

import jax
import jax.numpy as jnp
from jax import lax
from jax.sharding import PartitionSpec as P


def passed_along(block, axis, distance):
    devices = range(lax.axis_size(axis))
    route = [(i - distance, i) for i in devices if i - distance in devices]
    return lax.ppermute(block, axis, route)


def shards(signal, sketch):
    local_rows = signal.shape[0]
    channels = signal.shape[1]
    sketch_cols = sketch.shape[0]
    lag_count = sketch.shape[1] // channels
    samples_all = local_rows * lax.axis_size(("tx", "ty"))
    next_rows = passed_along(signal[: lag_count - 1], ("tx", "ty"), -1)
    extended = jnp.concatenate([signal, next_rows], axis=0)
    length = extended.shape[0]
    lagged = lax.dot_general(
        sketch.reshape(sketch_cols * lag_count, channels),
        extended,
        (((1,), (1,)), ((), ())),
        preferred_element_type=jnp.float32,
    )
    lagged = lagged.reshape(sketch_cols, lag_count, length)
    sketched = lagged[:, 0, 0:local_rows]
    for lag_index in range(1, lag_count):
        sketched = sketched + lagged[:, lag_index, lag_index : lag_index + local_rows]
    gram_local = jnp.dot(sketched, sketched.T, precision=lax.Precision.HIGHEST)
    gram = lax.psum(gram_local, ("tx", "ty")) / samples_all
    triangle = jnp.linalg.cholesky(gram)
    inverse = lax.linalg.triangular_solve(
        triangle, jnp.eye(sketch_cols, dtype=triangle.dtype), left_side=True, lower=True
    )
    basis_t = jnp.dot(inverse, sketched, precision=lax.Precision.HIGHEST)
    rounded = basis_t.astype(jnp.bfloat16)
    padded = jnp.pad(rounded, ((0, 0), (lag_count - 1, lag_count - 1)))
    shifted = jnp.stack(
        [
            padded[:, lag_count - 1 - lag_index : lag_count - 1 - lag_index + length]
            for lag_index in range(lag_count)
        ],
        axis=1,
    )
    partial_sum = jnp.dot(
        shifted.reshape(sketch_cols * lag_count, length),
        extended,
        preferred_element_type=jnp.float32,
    )
    partial_sum = partial_sum.reshape(sketch_cols, lag_count * channels)
    owned_sum = lax.psum_scatter(partial_sum, ("tx", "ty"), scatter_dimension=1, tiled=True)
    return (basis_t, owned_sum / math.sqrt(samples_all))


def solution(mesh):
    in_specs = (P(("tx", "ty"), None), P())
    out_specs = (P(None, ("tx", "ty")), P(None, ("tx", "ty")))
    return jax.shard_map(shards, mesh=mesh, in_specs=in_specs, out_specs=out_specs, check_vma=False)
```

profile of v0, /device:TPU:1, one launch (start us, length us, event | category | flops | bytes accessed | tf_op | source)
XLA Modules:
  0.0 1623.4 jit_solution(4681962879270737434)
XLA Ops:
  8.0 5.1 collective-permute-start
  14.2 2.9 reshape.31
  17.1 8.6 convolution_bitcast_fusion
  25.8 18.3 %copy.137 = f32[4096,1087]{1,0:T(8,128)} copy(f32[4096,1087]{0,1:T(8,128)} %convolution_bitcast_fusion) | data formatting | bytes 35618816 | tf_op jit(solution)/shard_map/dot_general | solution.py:24
  44.1 9.2 fusion.36
  53.2 25.8 %fusion.33 = (f32[64,1,1024]{2,1,0:T(1,128)}, f32[64,1,1024]{2,1,0:T(1,128)S(1)}, f32[64,1,1024]{2,1,0:T(1,128)S(1)}, f32[64,1,1024]{2,1,0:T(1,128)S(1)}, f32[64...) fusion(f32[64,64,1087]{2,1,0:T(8,128)} %bitcast.486), kind=kLoop, calls=%fused_computation.173 | loop fusion | bytes 9961472 | tf_op jit(solution)/shard_map/slice | solution.py:33
  79.1 26.5 %fusion.34 = (f32[64,1,1024]{2,1,0:T(1,128)}, f32[64,1,1024]{2,1,0:T(1,128)}, f32[64,1,1024]{2,1,0:T(1,128)}, f32[64,1,1024]{2,1,0:T(1,128)}, f32[64,1,1024]{2,1...) fusion(f32[64,64,1087]{2,1,0:T(8,128)} %bitcast.487), kind=kLoop, calls=%fused_computation.174 | loop fusion | bytes 9961472 | tf_op jit(solution)/shard_map/slice | solution.py:33
  105.5 25.0 %fusion.35 = (f32[64,1,1024]{2,1,0:T(1,128)}, f32[64,1,1024]{2,1,0:T(1,128)}, f32[64,1,1024]{2,1,0:T(1,128)}, f32[64,1,1024]{2,1,0:T(1,128)}, f32[64,1,1024]{2,1...) fusion(f32[64,64,1087]{2,1,0:T(8,128)} %bitcast.488), kind=kLoop, calls=%fused_computation.175 | loop fusion | bytes 9961472 | tf_op jit(solution)/shard_map/slice | solution.py:33
  130.9 1.9 copy.250
  132.7 1.2 copy.249
  133.9 1.1 copy.248
  135.0 1.1 copy.247
  136.1 1.1 copy.246
  137.2 1.1 copy.245
  138.4 1.1 copy.244
  139.5 1.1 copy.243
  140.6 1.1 copy.242
  141.7 1.1 copy.241
  142.8 1.1 copy.240
  143.9 1.1 copy.239
  149.4 1.1 copy.234
  154.2 2.2 add_add_fusion
  156.6 4.7 fusion.32
  161.7 81.3 %psum.7 = f32[64,64]{0,1:T(8,128)S(1)} all-reduce(f32[64,64]{0,1:T(8,128)S(1)} %fusion.3), channel_id=1, replica_groups=mesh['tx'=8,'ty'=32] {'tx','ty'}, use_global_device_ids=true, to_apply=%region_0.0 | all-reduce | flops 4096 | bytes 32768 | tf_op jit(solution)/shard_map/psum | solution.py:35
  243.1 5.8 cholesky.17
  250.3 4.9 custom-call.6
  255.4 6.7 fusion.37
  311.3 12.9 copy.203
  324.2 8.6 fusion.38
  332.8 4.9 reshape.34
  337.8 6.9 copy.205
  344.7 1270.2 %reduce-scatter.4.cloned.1.call-done = f32[64,64]{1,0:T(8,128)} async-done(((f32[16384,64]{1,0:T(8,128)}), f32[64,64]{1,0:T(8,128)}) %reduce-scatter.4.cloned.1.call-update) | async-done | bytes 16400
  (209 shorter events, 62.3 us)
Async XLA Ops:
  7.2 1607.7 %reduce-scatter.4.cloned.1.call-start = ((), (), s32[]{:S(2)}) async-start(), calls=%async_computation.1 | async-start | bytes 8421376
  8.0 9.1 collective-permute-start
  79.0 75.1 %copy-start = (f32[64,1,1024]{2,1,0:T(1,128)}, f32[64,1,1024]{2,1,0:T(1,128)S(1)}, u32[]{:S(2)}) copy-start(f32[64,1,1024]{2,1,0:T(1,128)S(1)} %get-tuple-element.17) | copy-start | bytes 786436
  79.0 75.1 %copy-start.1 = (f32[64,1,1024]{2,1,0:T(1,128)}, f32[64,1,1024]{2,1,0:T(1,128)S(1)}, u32[]{:S(2)}) copy-start(f32[64,1,1024]{2,1,0:T(1,128)S(1)} %get-tuple-element.18) | copy-start | bytes 786436
  79.0 75.1 %copy-start.2 = (f32[64,1,1024]{2,1,0:T(1,128)}, f32[64,1,1024]{2,1,0:T(1,128)S(1)}, u32[]{:S(2)}) copy-start(f32[64,1,1024]{2,1,0:T(1,128)S(1)} %get-tuple-element.19) | copy-start | bytes 786436
  79.0 75.1 %copy-start.3 = (f32[64,1,1024]{2,1,0:T(1,128)}, f32[64,1,1024]{2,1,0:T(1,128)S(1)}, u32[]{:S(2)}) copy-start(f32[64,1,1024]{2,1,0:T(1,128)S(1)} %get-tuple-element.20) | copy-start | bytes 786436
  79.0 75.1 %copy-start.4 = (f32[64,1,1024]{2,1,0:T(1,128)}, f32[64,1,1024]{2,1,0:T(1,128)S(1)}, u32[]{:S(2)}) copy-start(f32[64,1,1024]{2,1,0:T(1,128)S(1)} %get-tuple-element.21) | copy-start | bytes 786436
  79.0 75.1 %copy-start.5 = (f32[64,1,1024]{2,1,0:T(1,128)}, f32[64,1,1024]{2,1,0:T(1,128)S(1)}, u32[]{:S(2)}) copy-start(f32[64,1,1024]{2,1,0:T(1,128)S(1)} %get-tuple-element.22) | copy-start | bytes 786436
  130.6 22.1 %copy-start.53 = (f32[64,1,1024]{2,1,0:T(1,128)S(1)}, f32[64,1,1024]{2,1,0:T(1,128)}, u32[]{:S(2)}) copy-start(f32[64,1,1024]{2,1,0:T(1,128)} %get-tuple-element.48) | copy-start | bytes 786436
  130.6 22.2 %copy-start.52 = (f32[64,1,1024]{2,1,0:T(1,128)S(1)}, f32[64,1,1024]{2,1,0:T(1,128)}, u32[]{:S(2)}) copy-start(f32[64,1,1024]{2,1,0:T(1,128)} %get-tuple-element.49) | copy-start | bytes 786436
  130.6 22.2 %copy-start.35 = (f32[64,1,1024]{2,1,0:T(1,128)S(1)}, f32[64,1,1024]{2,1,0:T(1,128)}, u32[]{:S(2)}) copy-start(f32[64,1,1024]{2,1,0:T(1,128)} %get-tuple-element.62) | copy-start | bytes 786436
  130.7 22.2 %copy-start.36 = (f32[64,1,1024]{2,1,0:T(1,128)S(1)}, f32[64,1,1024]{2,1,0:T(1,128)}, u32[]{:S(2)}) copy-start(f32[64,1,1024]{2,1,0:T(1,128)} %get-tuple-element.63) | copy-start | bytes 786436
  130.7 22.2 %copy-start.37 = (f32[64,1,1024]{2,1,0:T(1,128)S(1)}, f32[64,1,1024]{2,1,0:T(1,128)}, u32[]{:S(2)}) copy-start(f32[64,1,1024]{2,1,0:T(1,128)} %get-tuple-element.64) | copy-start | bytes 786436
  130.7 22.2 %copy-start.38 = (f32[64,1,1024]{2,1,0:T(1,128)S(1)}, f32[64,1,1024]{2,1,0:T(1,128)}, u32[]{:S(2)}) copy-start(f32[64,1,1024]{2,1,0:T(1,128)} %get-tuple-element.65) | copy-start | bytes 786436
  130.7 22.2 %copy-start.39 = (f32[64,1,1024]{2,1,0:T(1,128)S(1)}, f32[64,1,1024]{2,1,0:T(1,128)}, u32[]{:S(2)}) copy-start(f32[64,1,1024]{2,1,0:T(1,128)} %get-tuple-element.66) | copy-start | bytes 786436
  130.7 22.2 %copy-start.40 = (f32[64,1,1024]{2,1,0:T(1,128)S(1)}, f32[64,1,1024]{2,1,0:T(1,128)}, u32[]{:S(2)}) copy-start(f32[64,1,1024]{2,1,0:T(1,128)} %get-tuple-element.50) | copy-start | bytes 786436
  130.7 22.2 %copy-start.41 = (f32[64,1,1024]{2,1,0:T(1,128)S(1)}, f32[64,1,1024]{2,1,0:T(1,128)}, u32[]{:S(2)}) copy-start(f32[64,1,1024]{2,1,0:T(1,128)} %get-tuple-element.51) | copy-start | bytes 786436
  130.7 22.2 %copy-start.42 = (f32[64,1,1024]{2,1,0:T(1,128)S(1)}, f32[64,1,1024]{2,1,0:T(1,128)}, u32[]{:S(2)}) copy-start(f32[64,1,1024]{2,1,0:T(1,128)} %get-tuple-element.52) | copy-start | bytes 786436
  130.7 22.2 %copy-start.43 = (f32[64,1,1024]{2,1,0:T(1,128)S(1)}, f32[64,1,1024]{2,1,0:T(1,128)}, u32[]{:S(2)}) copy-start(f32[64,1,1024]{2,1,0:T(1,128)} %get-tuple-element.53) | copy-start | bytes 786436
  130.7 22.2 %copy-start.44 = (f32[64,1,1024]{2,1,0:T(1,128)S(1)}, f32[64,1,1024]{2,1,0:T(1,128)}, u32[]{:S(2)}) copy-start(f32[64,1,1024]{2,1,0:T(1,128)} %get-tuple-element.54) | copy-start | bytes 786436
  130.7 22.2 %copy-start.45 = (f32[64,1,1024]{2,1,0:T(1,128)S(1)}, f32[64,1,1024]{2,1,0:T(1,128)}, u32[]{:S(2)}) copy-start(f32[64,1,1024]{2,1,0:T(1,128)} %get-tuple-element.55) | copy-start | bytes 786436
  130.8 22.2 %copy-start.46 = (f32[64,1,1024]{2,1,0:T(1,128)S(1)}, f32[64,1,1024]{2,1,0:T(1,128)}, u32[]{:S(2)}) copy-start(f32[64,1,1024]{2,1,0:T(1,128)} %get-tuple-element.56) | copy-start | bytes 786436
  130.8 22.2 %copy-start.47 = (f32[64,1,1024]{2,1,0:T(1,128)S(1)}, f32[64,1,1024]{2,1,0:T(1,128)}, u32[]{:S(2)}) copy-start(f32[64,1,1024]{2,1,0:T(1,128)} %get-tuple-element.57) | copy-start | bytes 786436
  130.8 22.2 %copy-start.48 = (f32[64,1,1024]{2,1,0:T(1,128)S(1)}, f32[64,1,1024]{2,1,0:T(1,128)}, u32[]{:S(2)}) copy-start(f32[64,1,1024]{2,1,0:T(1,128)} %get-tuple-element.58) | copy-start | bytes 786436
  130.8 22.2 %copy-start.49 = (f32[64,1,1024]{2,1,0:T(1,128)S(1)}, f32[64,1,1024]{2,1,0:T(1,128)}, u32[]{:S(2)}) copy-start(f32[64,1,1024]{2,1,0:T(1,128)} %get-tuple-element.59) | copy-start | bytes 786436
  130.8 22.2 %copy-start.50 = (f32[64,1,1024]{2,1,0:T(1,128)S(1)}, f32[64,1,1024]{2,1,0:T(1,128)}, u32[]{:S(2)}) copy-start(f32[64,1,1024]{2,1,0:T(1,128)} %get-tuple-element.60) | copy-start | bytes 786436
  130.8 22.2 %copy-start.51 = (f32[64,1,1024]{2,1,0:T(1,128)S(1)}, f32[64,1,1024]{2,1,0:T(1,128)}, u32[]{:S(2)}) copy-start(f32[64,1,1024]{2,1,0:T(1,128)} %get-tuple-element.61) | copy-start | bytes 786436
  130.8 23.3 %copy-start.6 = (f32[64,1,1024]{2,1,0:T(1,128)S(1)}, f32[64,1,1024]{2,1,0:T(1,128)}, u32[]{:S(2)}) copy-start(f32[64,1,1024]{2,1,0:T(1,128)} %get-tuple-element.23) | copy-start | bytes 786436
  130.8 23.3 %copy-start.7 = (f32[64,1,1024]{2,1,0:T(1,128)S(1)}, f32[64,1,1024]{2,1,0:T(1,128)}, u32[]{:S(2)}) copy-start(f32[64,1,1024]{2,1,0:T(1,128)} %get-tuple-element.25) | copy-start | bytes 786436
  130.8 23.3 %copy-start.8 = (f32[64,1,1024]{2,1,0:T(1,128)S(1)}, f32[64,1,1024]{2,1,0:T(1,128)}, u32[]{:S(2)}) copy-start(f32[64,1,1024]{2,1,0:T(1,128)} %get-tuple-element.43) | copy-start | bytes 786436
  130.8 23.3 %copy-start.10 = (f32[64,1,1024]{2,1,0:T(1,128)S(1)}, f32[64,1,1024]{2,1,0:T(1,128)}, u32[]{:S(2)}) copy-start(f32[64,1,1024]{2,1,0:T(1,128)} %get-tuple-element.5) | copy-start | bytes 786436
  133.9 22.5 %copy-start.11 = (f32[64,1,1024]{2,0,1:T(8,128)}, f32[64,1,1024]{2,0,1:T(8,128)S(1)}, u32[]{:S(2)}) copy-start(f32[64,1,1024]{2,0,1:T(8,128)S(1)} %copy.249) | copy-start | bytes 786436
  (28 other events, 364.1 us)
Sparse Core Ops, SparseCore 0:
  344.8 1270.0 reduce-scatter.3
where the time goes:
time: 1640 us; the launch traced here: 1620 us
  waiting for transfers between devices  1270 us (77%)
  local copies, waits for them, and re-layouts  206 us (13%)
  blocking collectives  81.3 us (5%)
  matrix products  24.6 us (2%)
  other arithmetic  20.6 us (1%)
    unnamed x2, waiting for transfers between devices  1270 us
    psum x1, blocking collectives, shards(): gram = lax.psum(gram_local, ('tx', 'ty')) / samples_all  81.3 us
    unnamed x207, local copies, waits for them, and re-layouts  79.1 us
    slice x3, local copies, waits for them, and re-layouts, shards(): sketched = sketched + lagged[:, lag_index, lag_index:lag_index + local_rows]  77.3 us
  transfers between devices with their start and end apart: 2, of which 1 were waited for; matrix products, arithmetic and copies ran while one was open for 0% of the time, Pallas kernels for 0%

commit v1 on v0

v1 whole, which is shorter than its diff:
```python
import math

import jax
import jax.numpy as jnp
from jax import lax
from jax.experimental import pallas as pl
from jax.experimental.pallas import tpu as pltpu
from jax.sharding import PartitionSpec as P

MESH = pl.DeviceIdType.MESH
F32 = jnp.float32
BF16 = jnp.bfloat16
HIGH = lax.Precision.HIGHEST
NT = (((1,), (1,)), ((), ()))

ROWS = 1024
CH = 256
RANK = 64
LAGS = 64
DEPTH = 2176
SAMPLES = 262144


def lower_inverse(gram):
    row_of = lax.broadcasted_iota(jnp.int32, (8, 128), 0)
    lane_of = lax.broadcasted_iota(jnp.int32, (8, 128), 1)
    blocks = []
    for g in range(8):
        eye = jnp.where(lane_of == row_of + (64 + 8 * g), 1.0, 0.0).astype(F32)
        blocks.append(jnp.concatenate([gram[8 * g : 8 * g + 8], eye[:, 64:]], axis=1))
    for k in range(RANK - 1):
        own, at = divmod(k, 8)
        row = blocks[own][at : at + 1, :]
        scaled = row / row[:, k : k + 1]
        for g in range(own, 8):
            col = blocks[g][:, k : k + 1]
            if g == own:
                col = jnp.where(row_of[:, 0:1] > at, col, 0.0)
            blocks[g] = blocks[g] - col * scaled
    out = []
    for g in range(8):
        pivot = jnp.sum(jnp.where(lane_of == row_of + 8 * g, blocks[g], 0.0), axis=1, keepdims=True)
        out.append(blocks[g][:, 64:] * (1.0 / jnp.sqrt(pivot)))
    return jnp.concatenate(out, axis=0)


def folded(block):
    return jnp.concatenate([block[0:32], block[32:64]], axis=1)


def unfolded(block):
    return jnp.concatenate([block[:, 0:64], block[:, 64:128]], axis=0)


def kernel(
    signal,
    sketch,
    basis,
    proj,
    sk_v,
    ext,
    xf,
    xs,
    pair,
    tail,
    pf,
    bs,
    uu,
    vv,
    skl,
    ss,
    gs,
    gx,
    gy,
    gz,
    ya,
    yb,
    ra,
    rb,
    sa,
    sb,
    r2a,
    r2b,
    zp,
    rz,
    local_sem,
    send_sem,
    recv_sem,
):
    z = lax.axis_index("tx")
    ty = lax.axis_index("ty")
    y = ty // 8
    x = (ty // 2) % 4
    core = ty % 2
    me = z * 32 + ty

    def along(offset):
        index = (me + offset + 256) % 256
        return (index // 32, index % 32)

    def x_peer(k):
        return (z, y * 8 + ((x + k + 4) % 4) * 2 + core)

    def y_peer(k):
        return (z, ((y + k + 4) % 4) * 8 + x * 2 + core)

    def z_peer(k):
        return ((z + k + 8) % 8, ty)

    twin = (z, ty + 1 - 2 * core)

    def own_quarters(rows):
        first = jnp.concatenate([rows[:, 0:64], rows[:, 128:192]], axis=1)
        second = jnp.concatenate([rows[:, 64:128], rows[:, 192:256]], axis=1)
        return jnp.where(core == 0, first, second)

    used = [0]

    def remote(src, dst, device):
        i = used[0]
        used[0] += 1
        return pltpu.make_async_remote_copy(
            src_ref=src,
            dst_ref=dst,
            send_sem=send_sem.at[i],
            recv_sem=recv_sem.at[i],
            device_id=device,
            device_id_type=MESH,
        )

    get_signal = pltpu.make_async_copy(signal, ext.at[pl.ds(0, ROWS)], local_sem.at[0])
    get_sketch = pltpu.make_async_copy(sketch, sk_v, local_sem.at[1])
    own_start = pl.multiple_of(core * ROWS, ROWS)
    twin_start = pl.multiple_of(ROWS - core * ROWS, ROWS)
    get_signal.start()
    get_sketch.start()

    barrier = pltpu.get_barrier_semaphore()
    sources = [along(1), along(2), twin]
    sources += [x_peer(-k) for k in range(1, 4)]
    sources += [y_peer(-k) for k in range(1, 4)]
    sources += [z_peer(-k) for k in range(1, 8)]
    for source in sources:
        pl.semaphore_signal(barrier, inc=1, device_id=source, device_id_type=MESH)
    pl.semaphore_wait(barrier, len(sources))

    halo_copy = remote(signal.at[pl.ds(0, 64)], ext.at[pl.ds(ROWS, 64)], along(-1))
    halo_copy.start()
    pair_copy = remote(signal, pair, twin)
    pair_copy.start()
    tail_copy = remote(signal.at[pl.ds(0, 64)], tail, along(-2))
    tail_copy.start()

    get_signal.wait()
    xf[pl.ds(1088, 64)] = jnp.zeros((64, CH), F32)

    @pl.loop(0, 16)
    def _(i):
        at = pl.multiple_of(i * 64, 64)
        xf[pl.ds(at, 64)] = ext[pl.ds(at, 64)].astype(F32)

    halo_copy.wait_recv()

    @pl.when(me == 255)
    def _():
        ext[pl.ds(ROWS, 64)] = jnp.zeros((64, CH), BF16)

    xf[pl.ds(ROWS, 64)] = ext[pl.ds(ROWS, 64)].astype(F32)

    @pl.loop(0, 17)
    def _(i):
        at = pl.multiple_of(i * 64, 64)
        near = xf[pl.ds(at, 80)]
        for m in range(1, 4):
            xs[m - 1, pl.ds(at, 64)] = near[4 * m : 4 * m + 64].astype(BF16)

    get_sketch.wait()
    span = 1040
    left = []
    for q in range(16):
        m, at = q % 4, 16 * (q // 4)
        left.append(ext[at : at + span] if m == 0 else xs[m - 1, at : at + span])
    right = [
        jnp.concatenate([sk_v[:, (4 * q + j) * CH : (4 * q + j + 1) * CH] for q in range(16)], axis=1)
        for j in range(4)
    ]
    uu[...] = lax.dot_general(
        jnp.concatenate(left, axis=1), jnp.concatenate(right, axis=0), NT, preferred_element_type=F32
    )
    vv[...] = uu[0:1032, 0:128] + uu[2:1034, 128:256]
    total = vv[0:ROWS] + pltpu.roll(vv[1 : ROWS + 1], 64, axis=1)
    skl[core] = total.T[0:RANK]
    sketched_copy = remote(skl.at[core], skl.at[core], twin)
    sketched_copy.start()

    pair_copy.wait_recv()
    tail_copy.wait_recv()
    last = jnp.where(core == 0, tail[...].astype(F32), xf[pl.ds(ROWS, 64)])
    pf[pl.ds(2048, 64)] = jnp.where(me >= 254, 0.0, own_quarters(last))
    pf[pl.ds(2112, 128)] = jnp.zeros((128, 128), F32)

    @pl.loop(0, 16)
    def _(i):
        at = pl.multiple_of(i * 64, 64)
        pf[pl.ds(own_start + at, 64)] = own_quarters(xf[pl.ds(at, 64)])
        pf[pl.ds(twin_start + at, 64)] = own_quarters(pair[pl.ds(at, 64)].astype(F32))

    @pl.loop(0, 137)
    def _(i):
        at = pl.multiple_of(i * 16, 16)
        near = pf[pl.ds(at, 64)]
        for m in range(4):
            now = near[4 * m : 4 * m + 16]
            later = near[4 * m + 32 : 4 * m + 48]
            low = jnp.concatenate([now[:, 0:64], later[:, 0:64]], axis=1)
            high = jnp.concatenate([now[:, 64:128], later[:, 64:128]], axis=1)
            bs[m, pl.ds(at, 16), 0:128] = low.astype(BF16)
            bs[m, pl.ds(at, 16), 128:256] = high.astype(BF16)

    sketched_copy.wait_recv()
    full = jnp.concatenate([skl[0], skl[1]], axis=1)
    gram = lax.dot_general(full, full, NT, precision=HIGH, preferred_element_type=F32)
    gs[0] = folded(gram)
    gram_x = [remote(gs.at[0], gx.at[k - 1], x_peer(k)) for k in range(1, 4)]
    for copy in gram_x:
        copy.start()

    padded = jnp.concatenate([full, jnp.zeros((RANK, DEPTH - 2048), F32)], axis=1)
    for j in range(4):
        moved = padded if j == 0 else pltpu.roll(padded, j, axis=1)
        high = moved.astype(BF16)
        ss[j * 64 : j * 64 + 64] = high
        ss[256 + j * 64 : 256 + j * 64 + 64] = (moved - high.astype(F32)).astype(BF16)

    def products(half, into):
        @pl.loop(0, 4)
        def _(m):
            both = jnp.dot(ss[...], bs[m, 16 * half : 16 * half + DEPTH], preferred_element_type=F32)
            block = both[0:256] + both[256:512]
            at = pl.ds(pl.multiple_of((m // 2) * 64, 64), 64)
            for j in range(4):
                y_to = (m % 2) * 2 + j // 2
                for x0 in range(2):
                    x_to = (j % 2) * 2 + x0
                    piece = block[j * 64 : j * 64 + 64, x0 * 128 : x0 * 128 + 128]
                    if half == 0:
                        into[x_to, y_to, at] = piece
                    else:
                        into[y_to, x_to, at] = piece

    products(0, ya)
    a_first = [remote(ya.at[(x + k) % 4], ra.at[k - 1], x_peer(k)) for k in range(1, 4)]
    for copy in a_first:
        copy.start()

    for copy in gram_x:
        copy.wait_recv()
    gs[1] = gs[0] + gx[0] + gx[1] + gx[2]
    gram_y = [remote(gs.at[1], gy.at[k - 1], y_peer(k)) for k in range(1, 4)]
    for copy in gram_y:
        copy.start()

    products(1, yb)
    b_first = [remote(yb.at[(y + k) % 4], rb.at[k - 1], y_peer(k)) for k in range(1, 4)]
    for copy in b_first:
        copy.start()

    for copy in gram_y:
        copy.wait_recv()
    gs[2] = gs[1] + gy[0] + gy[1] + gy[2]
    gram_z = [remote(gs.at[2], gz.at[k - 1], z_peer(k)) for k in range(1, 8)]
    for copy in gram_z:
        copy.start()
    for copy in gram_z:
        copy.wait_recv()
    gram_sum = gs[2]
    for k in range(7):
        gram_sum = gram_sum + gz[k]
    inverse = lower_inverse(unfolded(gram_sum) * (1.0 / SAMPLES))
    basis[...] = jnp.dot(inverse, skl[core], precision=HIGH, preferred_element_type=F32)

    for copy in a_first:
        copy.wait_recv()
    sa[...] = ya[x] + ra[0] + ra[1] + ra[2]
    a_second = [remote(sa.at[(y + k) % 4], r2a.at[k - 1], y_peer(k)) for k in range(1, 4)]
    for copy in a_second:
        copy.start()
    for copy in b_first:
        copy.wait_recv()
    sb[...] = yb[y] + rb[0] + rb[1] + rb[2]
    b_second = [remote(sb.at[(x + k) % 4], r2b.at[k - 1], x_peer(k)) for k in range(1, 4)]
    for copy in b_second:
        copy.start()

    def pack(l4, block):
        for l3 in range(2):
            top = block[l3 * 64 : l3 * 64 + 32]
            low = block[l3 * 64 + 32 : l3 * 64 + 64]
            zp[2 * l4 + l3] = jnp.concatenate([top[:, 0:64], low[:, 0:64]], axis=1)
            zp[4 + 2 * l4 + l3] = jnp.concatenate([top[:, 64:128], low[:, 64:128]], axis=1)

    for copy in a_second:
        copy.wait_recv()
    pack(0, sa[y] + r2a[0] + r2a[1] + r2a[2])
    for copy in b_second:
        copy.wait_recv()
    pack(1, sb[x] + r2b[0] + r2b[1] + r2b[2])
    last_copies = [remote(zp.at[(z + k) % 8], rz.at[k - 1], z_peer(k)) for k in range(1, 8)]
    for copy in last_copies:
        copy.start()
    for copy in last_copies:
        copy.wait_recv()
    owned = zp[z]
    for k in range(7):
        owned = owned + rz[k]
    proj[...] = jnp.dot(inverse, unfolded(owned), precision=HIGH, preferred_element_type=F32) * (
        1.0 / math.sqrt(SAMPLES)
    )

    sent = [halo_copy, pair_copy, tail_copy, sketched_copy]
    sent += gram_x + gram_y + gram_z + a_first + b_first + a_second + b_second + last_copies
    for copy in sent:
        copy.wait_send()


COPIES = 4 + 3 + 3 + 7 + 3 + 3 + 3 + 3 + 7


def shards(signal, sketch):
    return pl.pallas_call(
        kernel,
        out_shape=(
            jax.ShapeDtypeStruct((RANK, ROWS), F32),
            jax.ShapeDtypeStruct((RANK, 64), F32),
        ),
        in_specs=[pl.BlockSpec(memory_space=pl.ANY)] * 2,
        out_specs=[pl.BlockSpec(memory_space=pltpu.VMEM)] * 2,
        scratch_shapes=[
            pltpu.VMEM((RANK, LAGS * CH), BF16),
            pltpu.VMEM((1088, CH), BF16),
            pltpu.VMEM((1152, CH), F32),
            pltpu.VMEM((3, 1088, CH), BF16),
            pltpu.VMEM((ROWS, CH), BF16),
            pltpu.VMEM((64, CH), BF16),
            pltpu.VMEM((2240, 128), F32),
            pltpu.VMEM((4, 2192, CH), BF16),
            pltpu.VMEM((1040, CH), F32),
            pltpu.VMEM((1032, 128), F32),
            pltpu.VMEM((2, RANK, ROWS), F32),
            pltpu.VMEM((512, DEPTH), BF16),
            pltpu.VMEM((3, 32, 128), F32),
            pltpu.VMEM((3, 32, 128), F32),
            pltpu.VMEM((3, 32, 128), F32),
            pltpu.VMEM((7, 32, 128), F32),
            pltpu.VMEM((4, 4, 128, 128), F32),
            pltpu.VMEM((4, 4, 128, 128), F32),
            pltpu.VMEM((3, 4, 128, 128), F32),
            pltpu.VMEM((3, 4, 128, 128), F32),
            pltpu.VMEM((4, 128, 128), F32),
            pltpu.VMEM((4, 128, 128), F32),
            pltpu.VMEM((3, 128, 128), F32),
            pltpu.VMEM((3, 128, 128), F32),
            pltpu.VMEM((8, 32, 128), F32),
            pltpu.VMEM((7, 32, 128), F32),
            pltpu.SemaphoreType.DMA((2,)),
            pltpu.SemaphoreType.DMA((COPIES,)),
            pltpu.SemaphoreType.DMA((COPIES,)),
        ],
        compiler_params=pltpu.CompilerParams(
            collective_id=0, has_side_effects=True, vmem_limit_bytes=48 * 2**20
        ),
        name="range_finder",
    )(signal, sketch)


def solution(mesh):
    in_specs = (P(("tx", "ty"), None), P())
    out_specs = (P(None, ("tx", "ty")), P(None, ("tx", "ty")))
    return jax.shard_map(shards, mesh=mesh, in_specs=in_specs, out_specs=out_specs, check_vma=False)
```

time: 1640 us -> 66.8 us (0.04); the launches traced: 1620 us -> 66.7 us
  waiting for transfers between devices: 1270 us -> 0 us
  local copies, waits for them, and re-layouts: 206 us -> 3.94 us
  blocking collectives: 81.3 us -> 0 us
  Pallas kernels: 0 us -> 62.1 us
  matrix products: 24.6 us -> 0 us
  other arithmetic: 20.6 us -> 0 us
    unnamed x2 -> x0, waiting for transfers between devices: 1270 us -> none
    slice x5 -> x0, local copies, waits for them, and re-layouts: 87.2 us -> none  [the longest x3 77.3 us: shards(): sketched = sketched + lagged[:, lag_index, lag_index:lag_index + local_rows]]
    psum x1 -> x0, blocking collectives: 81.3 us -> none  [shards(): gram = lax.psum(gram_local, ('tx', 'ty')) / samples_all]
    unnamed x207 -> x6, local copies, waits for them, and re-layouts: 79.1 us -> 3.94 us
    pallas_call x0 -> x1, Pallas kernels: none -> 62.1 us  [shards(): pl.pallas_call(kernel, out_shape=(jax.ShapeDtypeStruct((RANK, ROWS), F32)...]
    dot_general x4 -> x0, matrix products: 24.4 us -> none  [the longest x1 8.64 us: shards(): lax.dot_general(sketch.reshape(sketch_cols * lag_count, channels), extend...]
    dot_general x1 -> x0, local copies, waits for them, and re-layouts: 18.3 us -> none  [shards(): lax.dot_general(sketch.reshape(sketch_cols * lag_count, channels), extend...]
  transfers between devices with their start and end apart: 2 -> 0, of which waited for: 1 -> 0; matrix products, arithmetic and copies ran while one was open for 0% -> 0% of each run, Pallas kernels for 0% -> 0%
where the time goes in v1:
time: 66.8 us; the launch traced here: 66.7 us
  Pallas kernels  62.1 us (93%)
  local copies, waits for them, and re-layouts  3.94 us (6%)
    pallas_call x1, Pallas kernels, shards(): pl.pallas_call(kernel, out_shape=(jax.ShapeDtypeStruct((RANK, ROWS), F32)...  62.1 us
    unnamed x6, local copies, waits for them, and re-layouts  3.94 us

profile of v1, /device:TPU:1, one launch (start us, length us, event | category | flops | bytes accessed | tf_op | source)
XLA Modules:
  0.0 66.7 jit_solution(3732344527560265609)
XLA Ops:
  0.6 0.0 copy-start
  0.6 1.6 %copy-done = bf16[64,16384]{1,0:T(8,128)(2,1)S(1)} copy-done((bf16[64,16384]{1,0:T(8,128)(2,1)S(1)}, bf16[64,16384]{1,0:T(8,128)(2,1)}, u32[]{:S(2)}) %copy-start) | copy-done | bytes 2097176
  2.2 0.0 copy-start.1
  2.2 1.0 %copy-done.1 = bf16[1024,256]{1,0:T(8,128)(2,1)S(1)} copy-done((bf16[1024,256]{1,0:T(8,128)(2,1)S(1)}, bf16[1024,256]{1,0:T(8,128)(2,1)}, u32[]{:S(2)}) %copy-start.1) | copy-done | bytes 524312
  3.3 62.1 %range_finder.1 = (f32[64,1024]{1,0:T(8,128)S(1)}, f32[64,64]{1,0:T(8,128)S(1)}) custom-call(bf16[1024,256]{1,0:T(8,128)(2,1)S(1)} %copy-done.1, bf16[64,16384]{1,0:T(8,128)(2,1)S(1)} %copy-done), custom_call_target="tpu_custom_call" | custom-call | tf_op jit(solution)/shard_map/range_finder/pallas_call | solution.py:330
  65.4 0.7 %copy.6 = f32[64,1024]{1,0:T(8,128)} copy(f32[64,1024]{1,0:T(8,128)S(1)} %get-tuple-element.4) | data formatting | bytes 524288
  66.1 0.6 copy.7
Async XLA Ops:
  0.6 1.6 %copy-start = (bf16[64,16384]{1,0:T(8,128)(2,1)S(1)}, bf16[64,16384]{1,0:T(8,128)(2,1)}, u32[]{:S(2)}) copy-start(bf16[64,16384]{1,0:T(8,128)(2,1)} %sketch.1) | copy-start | bytes 6291460
  2.2 1.0 %copy-start.1 = (bf16[1024,256]{1,0:T(8,128)(2,1)S(1)}, bf16[1024,256]{1,0:T(8,128)(2,1)}, u32[]{:S(2)}) copy-start(bf16[1024,256]{1,0:T(8,128)(2,1)} %signal.1) | copy-start | bytes 1572868

commit v2 on v1

v2 whole, which is shorter than its diff:
```python
import math

import jax
import jax.numpy as jnp
from jax import lax
from jax.experimental import pallas as pl
from jax.experimental.pallas import tpu as pltpu
from jax.sharding import PartitionSpec as P

MESH = pl.DeviceIdType.MESH
F32 = jnp.float32
BF16 = jnp.bfloat16
HIGH = lax.Precision.HIGHEST
NT = (((1,), (1,)), ((), ()))

ROWS = 1024
CH = 256
RANK = 64
LAGS = 64
HALF = 32
TIMES = 2048
DEPTH = 2176
SAMPLES = 262144


def lower_inverse(gram):
    row_of = lax.broadcasted_iota(jnp.int32, (8, 128), 0)
    lane_of = lax.broadcasted_iota(jnp.int32, (8, 128), 1)
    blocks = []
    for g in range(8):
        eye = jnp.where(lane_of == row_of + (64 + 8 * g), 1.0, 0.0).astype(F32)
        blocks.append(jnp.concatenate([gram[8 * g : 8 * g + 8], eye[:, 64:]], axis=1))
    for k in range(RANK - 1):
        own, at = divmod(k, 8)
        row = blocks[own][at : at + 1, :]
        scaled = row / row[:, k : k + 1]
        for g in range(own, 8):
            col = blocks[g][:, k : k + 1]
            if g == own:
                col = jnp.where(row_of[:, 0:1] > at, col, 0.0)
            blocks[g] = blocks[g] - col * scaled
    out = []
    for g in range(8):
        pivot = jnp.sum(jnp.where(lane_of == row_of + 8 * g, blocks[g], 0.0), axis=1, keepdims=True)
        out.append(blocks[g][:, 64:] * (1.0 / jnp.sqrt(pivot)))
    return jnp.concatenate(out, axis=0)


def folded(block):
    n = block.shape[0] // 2
    return jnp.concatenate([block[0:n], block[n:]], axis=1)


def unfolded(block):
    return jnp.concatenate([block[:, 0:64], block[:, 64:128]], axis=0)


class RingSum:
    def __init__(self, remote, blocks, place, right, left, passing, arrived):
        self.blocks, self.place, self.passing, self.arrived = blocks, place, passing, arrived
        self.after, self.before = (place + 1) % 4, (place + 3) % 4
        across = (place + 2) % 4
        self.across_first = remote(blocks.at[across, 0], passing.at[0], right)
        self.across_second = remote(blocks.at[across, 1], passing.at[1], left)
        self.before_first = remote(blocks.at[self.before, 0], arrived.at[1, 0], left)
        self.after_second = remote(blocks.at[self.after, 1], arrived.at[0, 1], right)
        self.after_first = remote(blocks.at[self.after, 0], arrived.at[0, 0], right)
        self.before_second = remote(blocks.at[self.before, 1], arrived.at[1, 1], left)

    def start_first(self):
        self.across_first.start()
        self.before_first.start()

    def start_second(self):
        self.across_second.start()
        self.after_second.start()

    def forward_first(self):
        self.across_first.wait_recv()
        self.blocks[self.after, 0] += self.passing[0]
        self.after_first.start()

    def forward_second(self):
        self.across_second.wait_recv()
        self.blocks[self.before, 1] += self.passing[1]
        self.before_second.start()

    def total_first(self):
        self.before_first.wait_recv()
        self.after_first.wait_recv()
        return self.blocks[self.place, 0] + self.arrived[0, 0] + self.arrived[1, 0]

    def total_second(self):
        self.after_second.wait_recv()
        self.before_second.wait_recv()
        return self.blocks[self.place, 1] + self.arrived[0, 1] + self.arrived[1, 1]


def kernel(
    signal,
    sketch,
    basis,
    proj,
    sk_v,
    xr,
    uu,
    vv,
    vw,
    skl,
    ss,
    gs,
    gx,
    gy,
    gz,
    ya,
    yb,
    fa,
    fb,
    ra,
    rb,
    sa,
    sb,
    ra2,
    rb2,
    zp,
    rz,
    local_sem,
    send_sem,
    recv_sem,
):
    z = lax.axis_index("tx")
    ty = lax.axis_index("ty")
    y = ty // 8
    x = (ty // 2) % 4
    core = ty % 2
    me = z * 32 + ty

    def along(offset):
        index = (me + offset + 256) % 256
        return (index // 32, index % 32)

    def x_peer(k):
        return (z, y * 8 + ((x + k + 4) % 4) * 2 + core)

    def y_peer(k):
        return (z, ((y + k + 4) % 4) * 8 + x * 2 + core)

    def z_peer(k):
        return ((z + k + 8) % 8, ty)

    other = ty + 1 - 2 * core
    twin = (z, other)

    def z_other(k):
        return ((z + k + 8) % 8, other)

    copies = []

    def remote(src, dst, device):
        i = len(copies)
        copies.append(pltpu.make_async_remote_copy(
            src_ref=src,
            dst_ref=dst,
            send_sem=send_sem.at[i],
            recv_sem=recv_sem.at[i],
            device_id=device,
            device_id_type=MESH,
        ))
        return copies[i]

    own_rows = pl.ds(pl.multiple_of(core * ROWS, ROWS), ROWS)
    own_ranks = pl.ds(pl.multiple_of(core * HALF, HALF), HALF)
    get_signal = pltpu.make_async_copy(signal, xr.at[0, own_rows], local_sem.at[0])
    get_sketch = pltpu.make_async_copy(sketch.at[own_ranks], sk_v, local_sem.at[1])
    get_signal.start()
    get_sketch.start()

    barrier = pltpu.get_barrier_semaphore()
    sources = [along(2 - core), twin]
    sources += [x_peer(-k) for k in range(1, 4)]
    sources += [y_peer(-k) for k in range(1, 4)]
    sources += [z_peer(-k) for k in range(1, 8)]
    sources += [z_other(-k) for k in range(1, 8)]
    for source in sources:
        pl.semaphore_signal(barrier, inc=1, device_id=source, device_id_type=MESH)
    pl.semaphore_wait(barrier, len(sources) - 1 + 2 * (1 - core))

    halo_rows = pl.ds(TIMES, 64)
    halo_near = remote(signal.at[pl.ds(0, 64)], xr.at[0, halo_rows], along(-1))
    halo_far = pltpu.make_async_remote_copy(
        src_ref=signal.at[pl.ds(0, 64)],
        dst_ref=xr.at[0, halo_rows],
        send_sem=local_sem.at[2],
        recv_sem=recv_sem.at[0],
        device_id=along(-2),
        device_id_type=MESH,
    )

    @pl.when(core == 0)
    def _():
        halo_near.start()
        halo_far.start()

    pair_copy = remote(signal, xr.at[0, own_rows], twin)
    pair_copy.start()

    for m in range(2):
        xr[m, 2112:2240] = jnp.zeros((128, CH), BF16)
    get_signal.wait()
    pair_copy.wait_recv()

    @pl.loop(0, 15)
    def _(i):
        at = pl.multiple_of(i * 128, 128)
        near = xr[0, pl.ds(at, 144)]
        xr[1, pl.ds(at, 128)] = near[8:136]

    near = xr[0, 1920:2048]
    xr[1, 1920:2032] = near[8:120]

    get_sketch.wait()
    columns = jnp.concatenate(
        [
            jnp.concatenate([sk_v[:, (8 * q + j) * CH : (8 * q + j + 1) * CH] for q in range(8)], axis=1)
            for j in range(8)
        ],
        axis=0,
    )

    def sub_shifted(start, rows):
        moved = [xr[q % 2, 16 * (q // 2) + start : 16 * (q // 2) + start + rows] for q in range(8)]
        uu[start : start + rows] = lax.dot_general(
            jnp.concatenate(moved, axis=1), columns, NT, preferred_element_type=F32
        )

    sub_shifted(0, 1984)
    halo_near.wait_recv()

    @pl.when(me >= 254)
    def _():
        xr[0, halo_rows] = jnp.zeros((64, CH), BF16)

    near = xr[0, 2032:2128]
    xr[1, 2032:2112] = near[8:88]
    sub_shifted(1984, 80)

    vv[...] = uu[0:2056, 0:128] + uu[4:2060, 128:256]
    vw[...] = vv[0:2052] + pltpu.roll(vv[2:2054], 64, axis=1)
    group = lax.broadcasted_iota(jnp.int32, (512, 128), 1) // HALF
    merged = None
    for g in range(4):
        at = g * 512
        part = vw[at : at + 512] + pltpu.roll(vw[at + 1 : at + 513], 96, axis=1)
        merged = part if g == 0 else jnp.where(group == g, pltpu.roll(part, 32 * g, axis=1), merged)
    turned = merged.T
    for g in range(4):
        skl[core, :, g * 512 : g * 512 + 512] = turned[g * HALF : g * HALF + HALF]
    sketched_copy = remote(skl.at[core], skl.at[core], twin)
    sketched_copy.start()

    padded = jnp.concatenate([skl[core], jnp.zeros((HALF, DEPTH - TIMES), F32)], axis=1)
    for j in range(8):
        moved = padded if j == 0 else pltpu.roll(padded, j, axis=1)
        high = moved.astype(BF16)
        ss[j * HALF : j * HALF + HALF] = high
        ss[256 + j * HALF : 256 + j * HALF + HALF] = (moved - high.astype(F32)).astype(BF16)

    def products(z_to, into, x_first):
        @pl.loop(0, 2)
        def _(i):
            right = xr[i, 8 * z_to : 8 * z_to + DEPTH]
            both = jnp.dot(ss[...], right, preferred_element_type=F32)
            block = both[0:256] + both[256:512]
            at = pl.ds(pl.multiple_of(i * HALF, HALF), HALF)
            half = (z_to % 4) // 2
            for j in range(8):
                y_to = j // 2
                for x0 in range(2):
                    x_to = (j % 2) * 2 + x0
                    piece = block[j * HALF : j * HALF + HALF, x0 * 128 : x0 * 128 + 128]
                    if x_first:
                        into[x_to, half, y_to, at] = piece
                    else:
                        into[y_to, half, x_to, at] = piece

    a_one = RingSum(remote, ya, x, x_peer(1), x_peer(-1), fa, ra)
    b_one = RingSum(remote, yb, y, y_peer(1), y_peer(-1), fb, rb)
    products(0, ya, True)
    a_one.start_first()
    products(4, yb, False)
    b_one.start_first()

    sketched_copy.wait_recv()
    full = jnp.concatenate([skl[0], skl[1]], axis=0)
    high = full.astype(BF16)
    rest = full - high.astype(F32)
    middle = rest.astype(BF16)
    low = (rest - middle.astype(F32)).astype(BF16)
    terms = jnp.concatenate([high, middle, low], axis=0)
    both = lax.dot_general(terms, terms, NT, preferred_element_type=F32)
    rows = both[0:64] + (both[64:128] + both[128:192])
    gs[0] = folded(rows[:, 0:64] + (rows[:, 64:128] + rows[:, 128:192]))
    gram_x = [remote(gs.at[0], gx.at[k - 1], x_peer(k)) for k in range(1, 4)]
    for copy in gram_x:
        copy.start()

    products(2, ya, True)
    a_one.start_second()
    products(6, yb, False)
    b_one.start_second()

    a_one.forward_first()
    for copy in gram_x:
        copy.wait_recv()
    gs[1] = gs[0] + gx[0] + gx[1] + gx[2]
    gram_y = [remote(gs.at[1], gy.at[k - 1], y_peer(k)) for k in range(1, 4)]
    for copy in gram_y:
        copy.start()
    b_one.forward_first()
    a_one.forward_second()
    b_one.forward_second()
    for copy in gram_y:
        copy.wait_recv()
    gs[2] = gs[1] + gy[0] + gy[1] + gy[2]
    gram_z = [remote(gs.at[2], gz.at[k - 1], z_peer(k)) for k in range(1, 8)]
    for copy in gram_z:
        copy.start()

    sa[:, 0] = a_one.total_first()
    sb[:, 0] = b_one.total_first()
    sa[:, 1] = a_one.total_second()
    a_two = [remote(sa.at[(y + k) % 4], ra2.at[k - 1], y_peer(k)) for k in range(1, 4)]
    for copy in a_two:
        copy.start()
    sb[:, 1] = b_one.total_second()
    b_two = [remote(sb.at[(x + k) % 4], rb2.at[k - 1], x_peer(k)) for k in range(1, 4)]
    for copy in b_two:
        copy.start()

    for copy in gram_z:
        copy.wait_recv()
    gram_sum = gs[2]
    for k in range(7):
        gram_sum = gram_sum + gz[k]
    inverse = lower_inverse(unfolded(gram_sum) * (1.0 / SAMPLES))

    def pack(z_to, halves):
        for h in range(2):
            for i in range(2):
                piece = halves[h][i * HALF : i * HALF + HALF]
                for c in range(2):
                    zp[z_to + 2 * h + i, c] = folded(piece[:, c * 64 : c * 64 + 64])

    for copy in a_two:
        copy.wait_recv()
    pack(0, [sa[y, h] + ra2[0, h] + ra2[1, h] + ra2[2, h] for h in range(2)])
    for copy in b_two:
        copy.wait_recv()
    pack(4, [sb[x, h] + rb2[0, h] + rb2[1, h] + rb2[2, h] for h in range(2)])
    last_copies = [remote(zp.at[z, 1 - core], rz.at[1, 0], twin)]
    for k in range(1, 8):
        last_copies.append(remote(zp.at[(z + k) % 8, core], rz.at[0, k], z_peer(k)))
        last_copies.append(remote(zp.at[(z + k) % 8, 1 - core], rz.at[1, k], z_other(k)))
    for copy in last_copies:
        copy.start()
    ours = pl.ds(pl.multiple_of(core * ROWS, ROWS), ROWS)
    basis[...] = jnp.dot(
        inverse,
        jnp.concatenate([skl[0, :, ours], skl[1, :, ours]], axis=0),
        precision=HIGH,
        preferred_element_type=F32,
    )
    for copy in last_copies:
        copy.wait_recv()
    own = zp[z, core]
    others = rz[1, 0]
    for k in range(1, 8):
        own = own + rz[0, k]
        others = others + rz[1, k]
    top = jnp.where(core == 0, own, others)
    bottom = jnp.where(core == 0, others, own)
    owned = jnp.concatenate([unfolded(top), unfolded(bottom)], axis=0)
    proj[...] = jnp.dot(inverse, owned, precision=HIGH, preferred_element_type=F32) * (1.0 / math.sqrt(SAMPLES))

    @pl.when(core == 0)
    def _():
        halo_near.wait_send()
        halo_far.wait_send()

    for copy in copies[1:]:
        copy.wait_send()


COPIES = 3 + 3 + 3 + 7 + 2 * 6 + 2 * 3 + 15


def shards(signal, sketch):
    return pl.pallas_call(
        kernel,
        out_shape=(
            jax.ShapeDtypeStruct((RANK, ROWS), F32),
            jax.ShapeDtypeStruct((RANK, 64), F32),
        ),
        in_specs=[pl.BlockSpec(memory_space=pl.ANY)] * 2,
        out_specs=[pl.BlockSpec(memory_space=pltpu.VMEM)] * 2,
        scratch_shapes=[
            pltpu.VMEM((HALF, LAGS * CH), BF16),
            pltpu.VMEM((2, 2240, CH), BF16),
            pltpu.VMEM((2064, CH), F32),
            pltpu.VMEM((2056, 128), F32),
            pltpu.VMEM((2052, 128), F32),
            pltpu.VMEM((2, HALF, TIMES), F32),
            pltpu.VMEM((512, DEPTH), BF16),
            pltpu.VMEM((3, 32, 128), F32),
            pltpu.VMEM((3, 32, 128), F32),
            pltpu.VMEM((3, 32, 128), F32),
            pltpu.VMEM((7, 32, 128), F32),
            pltpu.VMEM((4, 2, 4, 64, 128), F32),
            pltpu.VMEM((4, 2, 4, 64, 128), F32),
            pltpu.VMEM((2, 4, 64, 128), F32),
            pltpu.VMEM((2, 4, 64, 128), F32),
            pltpu.VMEM((2, 2, 4, 64, 128), F32),
            pltpu.VMEM((2, 2, 4, 64, 128), F32),
            pltpu.VMEM((4, 2, 64, 128), F32),
            pltpu.VMEM((4, 2, 64, 128), F32),
            pltpu.VMEM((3, 2, 64, 128), F32),
            pltpu.VMEM((3, 2, 64, 128), F32),
            pltpu.VMEM((8, 2, 16, 128), F32),
            pltpu.VMEM((2, 8, 16, 128), F32),
            pltpu.SemaphoreType.DMA((3,)),
            pltpu.SemaphoreType.DMA((COPIES,)),
            pltpu.SemaphoreType.DMA((COPIES,)),
        ],
        compiler_params=pltpu.CompilerParams(
            collective_id=0, has_side_effects=True, vmem_limit_bytes=63 * 2**20
        ),
        name="range_finder",
    )(signal, sketch)


def solution(mesh):
    in_specs = (P(("tx", "ty"), None), P())
    out_specs = (P(None, ("tx", "ty")), P(None, ("tx", "ty")))
    return jax.shard_map(shards, mesh=mesh, in_specs=in_specs, out_specs=out_specs, check_vma=False)
```

time: 66.8 us -> 52 us (0.78)
  Pallas kernels: 62.1 us -> 48.1 us
  local copies, waits for them, and re-layouts: 3.94 us -> 3.05 us
    pallas_call x1, Pallas kernels: 62.1 us -> 48.1 us  [shards(): pl.pallas_call(kernel, out_shape=(jax.ShapeDtypeStruct((RANK, ROWS), F32)...]
    unnamed x6 -> x2, local copies, waits for them, and re-layouts: 3.94 us -> 3.05 us
where the time goes in v2:
time: 52 us; the launch traced here: 51.8 us
  Pallas kernels  48.1 us (92%)
  local copies, waits for them, and re-layouts  3.05 us (6%)
  between operations  0.64 us (1%)
    pallas_call x1, Pallas kernels, shards(): pl.pallas_call(kernel, out_shape=(jax.ShapeDtypeStruct((RANK, ROWS), F32)...  48.1 us
    unnamed x2, local copies, waits for them, and re-layouts  3.05 us

profile of v2, /device:TPU:1, one launch (start us, length us, event | category | flops | bytes accessed | tf_op | source)
XLA Modules:
  0.0 51.8 jit_solution(3624751147154846563)
XLA Ops:
  0.6 48.1 %range_finder.1 = (f32[64,1024]{1,0:T(8,128)}, f32[64,64]{1,0:T(8,128)}) custom-call(bf16[1024,256]{1,0:T(8,128)(2,1)} %signal.1, bf16[64,16384]{1,0:T(8,128)(2,1)} %sketch.1), custom_call_target="tpu_custom_call" | custom-call | tf_op jit(solution)/shard_map/range_finder/pallas_call | solution.py:398
  48.8 1.7 %copy.6 = f32[64,1024]{1,0:T(8,128)} copy(f32[64,1024]{1,0:T(8,128)} %get-tuple-element.4) | data formatting | bytes 524288
  50.4 1.4 %copy.7 = f32[64,64]{1,0:T(8,128)} copy(f32[64,64]{1,0:T(8,128)} %get-tuple-element.5) | data formatting | bytes 32768

commit v3 on v2

--- a/solution.py
+++ b/solution.py
@@ -56,44 +56,37 @@
 
 
 class RingSum:
-    def __init__(self, remote, blocks, place, right, left, passing, arrived):
-        self.blocks, self.place, self.passing, self.arrived = blocks, place, passing, arrived
+    def __init__(self, remote, blocks, part, place, right, left, passing, arrived):
+        self.low, self.high = pl.ds(0, 2), pl.ds(2, 2)
+        self.blocks, self.part, self.place, self.passing, self.arrived = blocks, part, place, passing, arrived
         self.after, self.before = (place + 1) % 4, (place + 3) % 4
         across = (place + 2) % 4
-        self.across_first = remote(blocks.at[across, 0], passing.at[0], right)
-        self.across_second = remote(blocks.at[across, 1], passing.at[1], left)
-        self.before_first = remote(blocks.at[self.before, 0], arrived.at[1, 0], left)
-        self.after_second = remote(blocks.at[self.after, 1], arrived.at[0, 1], right)
-        self.after_first = remote(blocks.at[self.after, 0], arrived.at[0, 0], right)
-        self.before_second = remote(blocks.at[self.before, 1], arrived.at[1, 1], left)
-
-    def start_first(self):
-        self.across_first.start()
-        self.before_first.start()
-
-    def start_second(self):
-        self.across_second.start()
-        self.after_second.start()
-
-    def forward_first(self):
-        self.across_first.wait_recv()
-        self.blocks[self.after, 0] += self.passing[0]
-        self.after_first.start()
-
-    def forward_second(self):
-        self.across_second.wait_recv()
-        self.blocks[self.before, 1] += self.passing[1]
-        self.before_second.start()
-
-    def total_first(self):
-        self.before_first.wait_recv()
-        self.after_first.wait_recv()
-        return self.blocks[self.place, 0] + self.arrived[0, 0] + self.arrived[1, 0]
-
-    def total_second(self):
-        self.after_second.wait_recv()
-        self.before_second.wait_recv()
-        return self.blocks[self.place, 1] + self.arrived[0, 1] + self.arrived[1, 1]
+        low, high = (part, self.low), (part, self.high)
+        self.across_right = remote(blocks.at[(across, *low)], passing.at[part, 0], right)
+        self.across_left = remote(blocks.at[(across, *high)], passing.at[part, 1], left)
+        self.after_high = remote(blocks.at[(self.after, *high)], arrived.at[(0, *high)], right)
+        self.before_low = remote(blocks.at[(self.before, *low)], arrived.at[(1, *low)], left)
+        self.after_low = remote(blocks.at[(self.after, *low)], arrived.at[(0, *low)], right)
+        self.before_high = remote(blocks.at[(self.before, *high)], arrived.at[(1, *high)], left)
+
+    def start(self):
+        self.across_right.start()
+        self.across_left.start()
+        self.after_high.start()
+        self.before_low.start()
+
+    def forward(self):
+        self.across_right.wait_recv()
+        self.blocks[self.after, self.part, self.low] += self.passing[self.part, 0]
+        self.after_low.start()
+        self.across_left.wait_recv()
+        self.blocks[self.before, self.part, self.high] += self.passing[self.part, 1]
+        self.before_high.start()
+
+    def total(self):
+        for copy in (self.after_high, self.before_low, self.after_low, self.before_high):
+            copy.wait_recv()
+        return self.blocks[self.place, self.part] + self.arrived[0, self.part] + self.arrived[1, self.part]
 
 
 def kernel(
@@ -206,17 +199,19 @@
 
     for m in range(2):
         xr[m, 2112:2240] = jnp.zeros((128, CH), BF16)
+    def shifted(start, blocks, rest):
+        @pl.loop(0, blocks)
+        def _(i):
+            at = pl.multiple_of(start + i * 128, 16)
+            near = xr[0, pl.ds(at, 144)]
+            xr[1, pl.ds(at, 128)] = near[8:136]
+
+        at = pl.multiple_of(start + blocks * 128, 16)
+        near = xr[0, pl.ds(at, rest + 16)]
+        xr[1, pl.ds(at, rest)] = near[8 : 8 + rest]
+
     get_signal.wait()
-    pair_copy.wait_recv()
-
-    @pl.loop(0, 15)
-    def _(i):
-        at = pl.multiple_of(i * 128, 128)
-        near = xr[0, pl.ds(at, 144)]
-        xr[1, pl.ds(at, 128)] = near[8:136]
-
-    near = xr[0, 1920:2048]
-    xr[1, 1920:2032] = near[8:120]
+    shifted(core * ROWS, 7, 112)
 
     get_sketch.wait()
     columns = jnp.concatenate(
@@ -228,12 +223,15 @@
     )
 
     def sub_shifted(start, rows):
-        moved = [xr[q % 2, 16 * (q // 2) + start : 16 * (q // 2) + start + rows] for q in range(8)]
-        uu[start : start + rows] = lax.dot_general(
+        moved = [xr[q % 2, pl.ds(pl.multiple_of(16 * (q // 2) + start, 16), rows)] for q in range(8)]
+        uu[pl.ds(pl.multiple_of(start, 16), rows)] = lax.dot_general(
             jnp.concatenate(moved, axis=1), columns, NT, preferred_element_type=F32
         )
 
-    sub_shifted(0, 1984)
+    sub_shifted(core * ROWS, 960)
+    pair_copy.wait_recv()
+    shifted(ROWS - ROWS * core - 16 * (1 - core), 7, 128)
+    sub_shifted(960 - 960 * core, 1024)
     halo_near.wait_recv()
 
     @pl.when(me >= 254)
@@ -283,12 +281,12 @@
                     else:
                         into[y_to, half, x_to, at] = piece
 
-    a_one = RingSum(remote, ya, x, x_peer(1), x_peer(-1), fa, ra)
-    b_one = RingSum(remote, yb, y, y_peer(1), y_peer(-1), fb, rb)
+    a_one = [RingSum(remote, ya, part, x, x_peer(1), x_peer(-1), fa, ra) for part in range(2)]
+    b_one = [RingSum(remote, yb, part, y, y_peer(1), y_peer(-1), fb, rb) for part in range(2)]
     products(0, ya, True)
-    a_one.start_first()
+    a_one[0].start()
     products(4, yb, False)
-    b_one.start_first()
+    b_one[0].start()
 
     sketched_copy.wait_recv()
     full = jnp.concatenate([skl[0], skl[1]], axis=0)
@@ -305,44 +303,40 @@
         copy.start()
 
     products(2, ya, True)
-    a_one.start_second()
+    a_one[1].start()
     products(6, yb, False)
-    b_one.start_second()
-
-    a_one.forward_first()
+    b_one[1].start()
+
+    a_one[0].forward()
+    b_one[0].forward()
     for copy in gram_x:
         copy.wait_recv()
     gs[1] = gs[0] + gx[0] + gx[1] + gx[2]
     gram_y = [remote(gs.at[1], gy.at[k - 1], y_peer(k)) for k in range(1, 4)]
     for copy in gram_y:
         copy.start()
-    b_one.forward_first()
-    a_one.forward_second()
-    b_one.forward_second()
+    a_one[1].forward()
+    b_one[1].forward()
+
+    def second(ring, sums, place, peer, landing):
+        sums[:, ring.part] = ring.total()
+        sends = [
+            remote(sums.at[(place + k) % 4, ring.part], landing.at[k - 1, ring.part], peer(k)) for k in range(1, 4)
+        ]
+        for copy in sends:
+            copy.start()
+        return sends
+
+    a_two = second(a_one[0], sa, y, y_peer, ra2)
+    b_two = second(b_one[0], sb, x, x_peer, rb2)
     for copy in gram_y:
         copy.wait_recv()
     gs[2] = gs[1] + gy[0] + gy[1] + gy[2]
     gram_z = [remote(gs.at[2], gz.at[k - 1], z_peer(k)) for k in range(1, 8)]
     for copy in gram_z:
         copy.start()
-
-    sa[:, 0] = a_one.total_first()
-    sb[:, 0] = b_one.total_first()
-    sa[:, 1] = a_one.total_second()
-    a_two = [remote(sa.at[(y + k) % 4], ra2.at[k - 1], y_peer(k)) for k in range(1, 4)]
-    for copy in a_two:
-        copy.start()
-    sb[:, 1] = b_one.total_second()
-    b_two = [remote(sb.at[(x + k) % 4], rb2.at[k - 1], x_peer(k)) for k in range(1, 4)]
-    for copy in b_two:
-        copy.start()
-
-    for copy in gram_z:
-        copy.wait_recv()
-    gram_sum = gs[2]
-    for k in range(7):
-        gram_sum = gram_sum + gz[k]
-    inverse = lower_inverse(unfolded(gram_sum) * (1.0 / SAMPLES))
+    a_two += second(a_one[1], sa, y, y_peer, ra2)
+    b_two += second(b_one[1], sb, x, x_peer, rb2)
 
     def pack(z_to, halves):
         for h in range(2):
@@ -363,6 +357,13 @@
         last_copies.append(remote(zp.at[(z + k) % 8, 1 - core], rz.at[1, k], z_other(k)))
     for copy in last_copies:
         copy.start()
+
+    for copy in gram_z:
+        copy.wait_recv()
+    gram_sum = gs[2]
+    for k in range(7):
+        gram_sum = gram_sum + gz[k]
+    inverse = lower_inverse(unfolded(gram_sum) * (1.0 / SAMPLES))
     ours = pl.ds(pl.multiple_of(core * ROWS, ROWS), ROWS)
     basis[...] = jnp.dot(
         inverse,
@@ -391,7 +392,7 @@
         copy.wait_send()
 
 
-COPIES = 3 + 3 + 3 + 7 + 2 * 6 + 2 * 3 + 15
+COPIES = 3 + 3 + 3 + 7 + 4 * 6 + 4 * 3 + 15
 
 
 def shards(signal, sketch):
@@ -417,8 +418,8 @@
             pltpu.VMEM((7, 32, 128), F32),
             pltpu.VMEM((4, 2, 4, 64, 128), F32),
             pltpu.VMEM((4, 2, 4, 64, 128), F32),
-            pltpu.VMEM((2, 4, 64, 128), F32),
-            pltpu.VMEM((2, 4, 64, 128), F32),
+            pltpu.VMEM((2, 2, 2, 64, 128), F32),
+            pltpu.VMEM((2, 2, 2, 64, 128), F32),
             pltpu.VMEM((2, 2, 4, 64, 128), F32),
             pltpu.VMEM((2, 2, 4, 64, 128), F32),
             pltpu.VMEM((4, 2, 64, 128), F32),
@@ -432,7 +433,7 @@
             pltpu.SemaphoreType.DMA((COPIES,)),
         ],
         compiler_params=pltpu.CompilerParams(
-            collective_id=0, has_side_effects=True, vmem_limit_bytes=63 * 2**20
+            collective_id=0, has_side_effects=True, vmem_limit_bytes=54784 * 1024
         ),
         name="range_finder",
     )(signal, sketch)

time: 52 us -> 48.6 us (0.935); the launches traced: 51.8 us -> 47.9 us
  Pallas kernels: 48.1 us -> 45.9 us
  local copies, waits for them, and re-layouts: 3.05 us -> 1.32 us
    pallas_call x1, Pallas kernels: 48.1 us -> 45.9 us  [shards(): pl.pallas_call(kernel, out_shape=(jax.ShapeDtypeStruct((RANK, ROWS), F32)...]
    unnamed x2, local copies, waits for them, and re-layouts: 3.05 us -> 1.32 us
where the time goes in v3:
time: 48.6 us; the launch traced here: 47.9 us
  Pallas kernels  45.9 us (94%)
  local copies, waits for them, and re-layouts  1.32 us (3%)
  between operations  0.64 us (1%)
    pallas_call x1, Pallas kernels, shards(): pl.pallas_call(kernel, out_shape=(jax.ShapeDtypeStruct((RANK, ROWS), F32)...  45.9 us
    unnamed x2, local copies, waits for them, and re-layouts  1.32 us

profile of v3, /device:TPU:1, one launch (start us, length us, event | category | flops | bytes accessed | tf_op | source)
XLA Modules:
  0.0 47.9 jit_solution(7963256004650963916)
XLA Ops:
  0.6 45.9 %range_finder.1 = (f32[64,1024]{1,0:T(8,128)S(1)}, f32[64,64]{1,0:T(8,128)S(1)}) custom-call(bf16[1024,256]{1,0:T(8,128)(2,1)} %signal.1, bf16[64,16384]{1,0:T(8,128)(2,1)} %sketch.1), custom_call_target="tpu_custom_call" | custom-call | tf_op jit(solution)/shard_map/range_finder/pallas_call | solution.py:399
  46.5 0.7 %copy.6 = f32[64,1024]{1,0:T(8,128)} copy(f32[64,1024]{1,0:T(8,128)S(1)} %get-tuple-element.4) | data formatting | bytes 524288
  47.2 0.6 %copy.7 = f32[64,64]{1,0:T(8,128)} copy(f32[64,64]{1,0:T(8,128)S(1)} %get-tuple-element.5) | data formatting | bytes 32768

commit v4 on v3

--- a/solution.py
+++ b/solution.py
@@ -120,6 +120,8 @@
     local_sem,
     send_sem,
     recv_sem,
+    last_send,
+    last_recv,
 ):
     z = lax.axis_index("tx")
     ty = lax.axis_index("ty")
@@ -288,6 +290,11 @@
     products(4, yb, False)
     b_one[0].start()
 
+    products(2, ya, True)
+    a_one[1].start()
+    products(6, yb, False)
+    b_one[1].start()
+
     sketched_copy.wait_recv()
     full = jnp.concatenate([skl[0], skl[1]], axis=0)
     high = full.astype(BF16)
@@ -302,11 +309,6 @@
     for copy in gram_x:
         copy.start()
 
-    products(2, ya, True)
-    a_one[1].start()
-    products(6, yb, False)
-    b_one[1].start()
-
     a_one[0].forward()
     b_one[0].forward()
     for copy in gram_x:
@@ -345,18 +347,38 @@
                 for c in range(2):
                     zp[z_to + 2 * h + i, c] = folded(piece[:, c * 64 : c * 64 + 64])
 
+    def along_z(z_to):
+        k = (z_to - z + 8) % 8
+        pair = []
+        for which, device in ((0, (z_to, ty)), (1, (z_to, other))):
+            pair.append(pltpu.make_async_remote_copy(
+                src_ref=zp.at[z_to, (core + which) % 2],
+                dst_ref=rz.at[which, k],
+                send_sem=last_send.at[which, k],
+                recv_sem=last_recv.at[which, k],
+                device_id=device,
+                device_id_type=MESH,
+            ))
+        return pair
+
+    def send_along_z(first):
+        for z_to in range(first, first + 4):
+            same_core, other_core = along_z(z_to)
+
+            @pl.when(z != z_to)
+            def _():
+                same_core.start()
+
+            other_core.start()
+
     for copy in a_two:
         copy.wait_recv()
     pack(0, [sa[y, h] + ra2[0, h] + ra2[1, h] + ra2[2, h] for h in range(2)])
+    send_along_z(0)
     for copy in b_two:
         copy.wait_recv()
     pack(4, [sb[x, h] + rb2[0, h] + rb2[1, h] + rb2[2, h] for h in range(2)])
-    last_copies = [remote(zp.at[z, 1 - core], rz.at[1, 0], twin)]
-    for k in range(1, 8):
-        last_copies.append(remote(zp.at[(z + k) % 8, core], rz.at[0, k], z_peer(k)))
-        last_copies.append(remote(zp.at[(z + k) % 8, 1 - core], rz.at[1, k], z_other(k)))
-    for copy in last_copies:
-        copy.start()
+    send_along_z(4)
 
     for copy in gram_z:
         copy.wait_recv()
@@ -371,8 +393,11 @@
         precision=HIGH,
         preferred_element_type=F32,
     )
-    for copy in last_copies:
-        copy.wait_recv()
+    landed = [along_z((z + k) % 8) for k in range(8)]
+    for k in range(8):
+        if k > 0:
+            landed[k][0].wait_recv()
+        landed[k][1].wait_recv()
     own = zp[z, core]
     others = rz[1, 0]
     for k in range(1, 8):
@@ -390,9 +415,13 @@
 
     for copy in copies[1:]:
         copy.wait_send()
-
-
-COPIES = 3 + 3 + 3 + 7 + 4 * 6 + 4 * 3 + 15
+    for k in range(8):
+        if k > 0:
+            landed[k][0].wait_send()
+        landed[k][1].wait_send()
+
+
+COPIES = 3 + 3 + 3 + 7 + 4 * 6 + 4 * 3
 
 
 def shards(signal, sketch):
@@ -431,6 +460,8 @@
             pltpu.SemaphoreType.DMA((3,)),
             pltpu.SemaphoreType.DMA((COPIES,)),
             pltpu.SemaphoreType.DMA((COPIES,)),
+            pltpu.SemaphoreType.DMA((2, 8)),
+            pltpu.SemaphoreType.DMA((2, 8)),
         ],
         compiler_params=pltpu.CompilerParams(
             collective_id=0, has_side_effects=True, vmem_limit_bytes=54784 * 1024

time: 48.6 us -> 46.6 us (0.959)
  the two profiles are of different devices: /device:TPU:1 before, /device:TPU:6 now
where the time goes in v4:
time: 46.6 us; the launch traced here: 46.5 us
  Pallas kernels  44.6 us (96%)
  local copies, waits for them, and re-layouts  1.32 us (3%)
  between operations  0.64 us (1%)
    pallas_call x1, Pallas kernels, shards(): pl.pallas_call(kernel, out_shape=(jax.ShapeDtypeStruct((RANK, ROWS), F32)...  44.6 us
    unnamed x2, local copies, waits for them, and re-layouts  1.32 us

profile of v4, /device:TPU:6, one launch (start us, length us, event | category | flops | bytes accessed | tf_op | source)
XLA Modules:
  0.0 46.5 jit_solution(15427480837894928680)
XLA Ops:
  0.6 44.6 %range_finder.1 = (f32[64,1024]{1,0:T(8,128)S(1)}, f32[64,64]{1,0:T(8,128)S(1)}) custom-call(bf16[1024,256]{1,0:T(8,128)(2,1)} %signal.1, bf16[64,16384]{1,0:T(8,128)(2,1)} %sketch.1), custom_call_target="tpu_custom_call" | custom-call | tf_op jit(solution)/shard_map/range_finder/pallas_call | solution.py:428
  45.2 0.7 %copy.6 = f32[64,1024]{1,0:T(8,128)} copy(f32[64,1024]{1,0:T(8,128)S(1)} %get-tuple-element.4) | data formatting | bytes 524288
  45.9 0.6 %copy.7 = f32[64,64]{1,0:T(8,128)} copy(f32[64,64]{1,0:T(8,128)S(1)} %get-tuple-element.5) | data formatting | bytes 32768

commit v5 on v4

--- a/solution.py
+++ b/solution.py
@@ -57,35 +57,25 @@
 
 class RingSum:
     def __init__(self, remote, blocks, part, place, right, left, passing, arrived):
-        self.low, self.high = pl.ds(0, 2), pl.ds(2, 2)
         self.blocks, self.part, self.place, self.passing, self.arrived = blocks, part, place, passing, arrived
-        self.after, self.before = (place + 1) % 4, (place + 3) % 4
-        across = (place + 2) % 4
-        low, high = (part, self.low), (part, self.high)
-        self.across_right = remote(blocks.at[(across, *low)], passing.at[part, 0], right)
-        self.across_left = remote(blocks.at[(across, *high)], passing.at[part, 1], left)
-        self.after_high = remote(blocks.at[(self.after, *high)], arrived.at[(0, *high)], right)
-        self.before_low = remote(blocks.at[(self.before, *low)], arrived.at[(1, *low)], left)
-        self.after_low = remote(blocks.at[(self.after, *low)], arrived.at[(0, *low)], right)
-        self.before_high = remote(blocks.at[(self.before, *high)], arrived.at[(1, *high)], left)
+        forward, backward = (left, right) if part else (right, left)
+        self.ahead, behind = (place + (3 if part else 1)) % 4, (place + (1 if part else 3)) % 4
+        self.across = remote(blocks.at[(place + 2) % 4, part], passing.at[part], forward)
+        self.back = remote(blocks.at[behind, part], arrived.at[1, part], backward)
+        self.on = remote(blocks.at[self.ahead, part], arrived.at[0, part], forward)
 
     def start(self):
-        self.across_right.start()
-        self.across_left.start()
-        self.after_high.start()
-        self.before_low.start()
+        self.across.start()
+        self.back.start()
 
     def forward(self):
-        self.across_right.wait_recv()
-        self.blocks[self.after, self.part, self.low] += self.passing[self.part, 0]
-        self.after_low.start()
-        self.across_left.wait_recv()
-        self.blocks[self.before, self.part, self.high] += self.passing[self.part, 1]
-        self.before_high.start()
+        self.across.wait_recv()
+        self.blocks[self.ahead, self.part] += self.passing[self.part]
+        self.on.start()
 
     def total(self):
-        for copy in (self.after_high, self.before_low, self.after_low, self.before_high):
-            copy.wait_recv()
+        self.back.wait_recv()
+        self.on.wait_recv()
         return self.blocks[self.place, self.part] + self.arrived[0, self.part] + self.arrived[1, self.part]
 
 
@@ -202,8 +192,7 @@
     for m in range(2):
         xr[m, 2112:2240] = jnp.zeros((128, CH), BF16)
     def shifted(start, blocks, rest):
-        @pl.loop(0, blocks)
-        def _(i):
+        for i in range(blocks):
             at = pl.multiple_of(start + i * 128, 16)
             near = xr[0, pl.ds(at, 144)]
             xr[1, pl.ds(at, 128)] = near[8:136]
@@ -266,12 +255,11 @@
         ss[256 + j * HALF : 256 + j * HALF + HALF] = (moved - high.astype(F32)).astype(BF16)
 
     def products(z_to, into, x_first):
-        @pl.loop(0, 2)
-        def _(i):
+        for i in range(2):
             right = xr[i, 8 * z_to : 8 * z_to + DEPTH]
             both = jnp.dot(ss[...], right, preferred_element_type=F32)
             block = both[0:256] + both[256:512]
-            at = pl.ds(pl.multiple_of(i * HALF, HALF), HALF)
+            at = slice(i * HALF, i * HALF + HALF)
             half = (z_to % 4) // 2
             for j in range(8):
                 y_to = j // 2
@@ -320,25 +308,22 @@
     a_one[1].forward()
     b_one[1].forward()
 
-    def second(ring, sums, place, peer, landing):
-        sums[:, ring.part] = ring.total()
-        sends = [
-            remote(sums.at[(place + k) % 4, ring.part], landing.at[k - 1, ring.part], peer(k)) for k in range(1, 4)
-        ]
+    def second(rings, sums, place, peer, landing):
+        for ring in rings:
+            sums[:, ring.part] = ring.total()
+        sends = [remote(sums.at[(place + k) % 4], landing.at[k - 1], peer(k)) for k in (2, 1, 3)]
         for copy in sends:
             copy.start()
         return sends
 
-    a_two = second(a_one[0], sa, y, y_peer, ra2)
-    b_two = second(b_one[0], sb, x, x_peer, rb2)
     for copy in gram_y:
         copy.wait_recv()
     gs[2] = gs[1] + gy[0] + gy[1] + gy[2]
     gram_z = [remote(gs.at[2], gz.at[k - 1], z_peer(k)) for k in range(1, 8)]
     for copy in gram_z:
         copy.start()
-    a_two += second(a_one[1], sa, y, y_peer, ra2)
-    b_two += second(b_one[1], sb, x, x_peer, rb2)
+    a_two = second(a_one, sa, y, y_peer, ra2)
+    b_two = second(b_one, sb, x, x_peer, rb2)
 
     def pack(z_to, halves):
         for h in range(2):
@@ -421,7 +406,7 @@
         landed[k][1].wait_send()
 
 
-COPIES = 3 + 3 + 3 + 7 + 4 * 6 + 4 * 3
+COPIES = 3 + 3 + 3 + 7 + 4 * 3 + 2 * 3
 
 
 def shards(signal, sketch):
@@ -447,8 +432,8 @@
             pltpu.VMEM((7, 32, 128), F32),
             pltpu.VMEM((4, 2, 4, 64, 128), F32),
             pltpu.VMEM((4, 2, 4, 64, 128), F32),
-            pltpu.VMEM((2, 2, 2, 64, 128), F32),
-            pltpu.VMEM((2, 2, 2, 64, 128), F32),
+            pltpu.VMEM((2, 4, 64, 128), F32),
+            pltpu.VMEM((2, 4, 64, 128), F32),
             pltpu.VMEM((2, 2, 4, 64, 128), F32),
             pltpu.VMEM((2, 2, 4, 64, 128), F32),
             pltpu.VMEM((4, 2, 64, 128), F32),

time: 46.6 us -> 45.3 us (0.972)
  the two profiles are of different devices: /device:TPU:6 before, /device:TPU:32 now
where the time goes in v5:
time: 45.3 us; the launch traced here: 45.2 us
  Pallas kernels  43.2 us (95%)
  local copies, waits for them, and re-layouts  1.32 us (3%)
  between operations  0.64 us (1%)
    pallas_call x1, Pallas kernels, shards(): pl.pallas_call(kernel, out_shape=(jax.ShapeDtypeStruct((RANK, ROWS), F32)...  43.2 us
    unnamed x2, local copies, waits for them, and re-layouts  1.32 us

profile of v5, /device:TPU:32, one launch (start us, length us, event | category | flops | bytes accessed | tf_op | source)
XLA Modules:
  0.0 45.2 jit_solution(2881355190040666886)
XLA Ops:
  0.6 43.2 %range_finder.1 = (f32[64,1024]{1,0:T(8,128)S(1)}, f32[64,64]{1,0:T(8,128)S(1)}) custom-call(bf16[1024,256]{1,0:T(8,128)(2,1)} %signal.1, bf16[64,16384]{1,0:T(8,128)(2,1)} %sketch.1), custom_call_target="tpu_custom_call" | custom-call | tf_op jit(solution)/shard_map/range_finder/pallas_call | solution.py:413
  43.9 0.7 %copy.6 = f32[64,1024]{1,0:T(8,128)} copy(f32[64,1024]{1,0:T(8,128)S(1)} %get-tuple-element.4) | data formatting | bytes 524288
  44.6 0.6 %copy.7 = f32[64,64]{1,0:T(8,128)} copy(f32[64,64]{1,0:T(8,128)S(1)} %get-tuple-element.5) | data formatting | bytes 32768

commit v6 on v5

--- a/solution.py
+++ b/solution.py
@@ -409,13 +409,23 @@
 COPIES = 3 + 3 + 3 + 7 + 4 * 3 + 2 * 3
 
 
+def finish(basis, proj, basis_out, proj_out, sem):
+    first = pltpu.make_async_copy(basis, basis_out, sem.at[0])
+    second = pltpu.make_async_copy(proj, proj_out, sem.at[1])
+    first.start()
+    second.start()
+    first.wait()
+    second.wait()
+
+
 def shards(signal, sketch):
-    return pl.pallas_call(
+    shapes = (
+        jax.ShapeDtypeStruct((RANK, ROWS), F32),
+        jax.ShapeDtypeStruct((RANK, 64), F32),
+    )
+    results = pl.pallas_call(
         kernel,
-        out_shape=(
-            jax.ShapeDtypeStruct((RANK, ROWS), F32),
-            jax.ShapeDtypeStruct((RANK, 64), F32),
-        ),
+        out_shape=shapes,
         in_specs=[pl.BlockSpec(memory_space=pl.ANY)] * 2,
         out_specs=[pl.BlockSpec(memory_space=pltpu.VMEM)] * 2,
         scratch_shapes=[
@@ -453,6 +463,15 @@
         ),
         name="range_finder",
     )(signal, sketch)
+    return pl.pallas_call(
+        finish,
+        out_shape=shapes,
+        in_specs=[pl.BlockSpec(memory_space=pltpu.VMEM)] * 2,
+        out_specs=[pl.BlockSpec(memory_space=pltpu.HBM)] * 2,
+        scratch_shapes=[pltpu.SemaphoreType.DMA((2,))],
+        compiler_params=pltpu.CompilerParams(vmem_limit_bytes=2**20),
+        name="write_results",
+    )(*results)
 
 
 def solution(mesh):

time: 45.3 us -> 44.7 us (0.987)
  local copies, waits for them, and re-layouts: 1.32 us -> 0 us
  Pallas kernels: 43.2 us -> 44 us
    unnamed x2 -> x0, local copies, waits for them, and re-layouts: 1.32 us -> none
    pallas_call x1 -> x2, Pallas kernels: 43.2 us -> 44 us  [the longest x1 43.2 us: shards(): pl.pallas_call(kernel, out_shape=shapes, in_specs=[pl.BlockSpec(memory_sp...]
where the time goes in v6:
time: 44.7 us; the launch traced here: 44.6 us
  Pallas kernels  44 us (98%)
  between operations  0.64 us (1%)
    pallas_call x1, Pallas kernels, shards(): pl.pallas_call(kernel, out_shape=shapes, in_specs=[pl.BlockSpec(memory_sp...  43.2 us

profile of v6, /device:TPU:32, one launch (start us, length us, event | category | flops | bytes accessed | tf_op | source)
XLA Modules:
  0.0 44.6 jit_solution(1006237793129227078)
XLA Ops:
  0.6 43.2 %range_finder.1 = (f32[64,1024]{1,0:T(8,128)S(1)}, f32[64,64]{1,0:T(8,128)S(1)}) custom-call(bf16[1024,256]{1,0:T(8,128)(2,1)} %signal.1, bf16[64,16384]{1,0:T(8,128)(2,1)} %sketch.1), custom_call_target="tpu_custom_call" | custom-call | tf_op jit(solution)/shard_map/range_finder/pallas_call | solution.py:426
  43.9 0.7 %write_results.1 = (f32[64,1024]{1,0:T(8,128)}, f32[64,64]{1,0:T(8,128)}) custom-call(f32[64,1024]{1,0:T(8,128)S(1)} %get-tuple-element.4.basis, f32[64,64]{1,0:T(8,128)S(1)} %get-tuple-element.5.proj), custom_call_target="tpu_custom_call" | custom-call | tf_op jit(solution)/shard_map/write_results/pallas_call | solution.py:466

commit v7 on v6

--- a/solution.py
+++ b/solution.py
@@ -19,7 +19,7 @@
 LAGS = 64
 HALF = 32
 TIMES = 2048
-DEPTH = 2176
+DEPTH = 2304
 SAMPLES = 262144
 
 
@@ -190,7 +190,7 @@
     pair_copy.start()
 
     for m in range(2):
-        xr[m, 2112:2240] = jnp.zeros((128, CH), BF16)
+        xr[m, 2112:2368] = jnp.zeros((256, CH), BF16)
     def shifted(start, blocks, rest):
         for i in range(blocks):
             at = pl.multiple_of(start + i * 128, 16)
@@ -430,7 +430,7 @@
         out_specs=[pl.BlockSpec(memory_space=pltpu.VMEM)] * 2,
         scratch_shapes=[
             pltpu.VMEM((HALF, LAGS * CH), BF16),
-            pltpu.VMEM((2, 2240, CH), BF16),
+            pltpu.VMEM((2, 2368, CH), BF16),
             pltpu.VMEM((2064, CH), F32),
             pltpu.VMEM((2056, 128), F32),
             pltpu.VMEM((2052, 128), F32),

time: 44.7 us -> 44.7 us (level)
  no operation moved by 1% of the time
where the time goes in v7:
time: 44.7 us; the launch traced here: 44.6 us
  Pallas kernels  44 us (98%)
  between operations  0.64 us (1%)
    pallas_call x1, Pallas kernels, shards(): pl.pallas_call(kernel, out_shape=shapes, in_specs=[pl.BlockSpec(memory_sp...  43.3 us

profile of v7, /device:TPU:32, one launch (start us, length us, event | category | flops | bytes accessed | tf_op | source)
XLA Modules:
  0.0 44.6 jit_solution(12522492530387772661)
XLA Ops:
  0.6 43.3 %range_finder.1 = (f32[64,1024]{1,0:T(8,128)S(1)}, f32[64,64]{1,0:T(8,128)S(1)}) custom-call(bf16[1024,256]{1,0:T(8,128)(2,1)} %signal.1, bf16[64,16384]{1,0:T(8,128)(2,1)} %sketch.1), custom_call_target="tpu_custom_call" | custom-call | tf_op jit(solution)/shard_map/range_finder/pallas_call | solution.py:426
  43.9 0.7 %write_results.1 = (f32[64,1024]{1,0:T(8,128)}, f32[64,64]{1,0:T(8,128)}) custom-call(f32[64,1024]{1,0:T(8,128)S(1)} %get-tuple-element.4.basis, f32[64,64]{1,0:T(8,128)S(1)} %get-tuple-element.5.proj), custom_call_target="tpu_custom_call" | custom-call | tf_op jit(solution)/shard_map/write_results/pallas_call | solution.py:466
